TPU v7x, 128 devices: a whole 4x4x4 slice. The times are simulated.
128 devices in a mesh: dp: 16 (over y_lo, x, core), fsdp: 8 (over y_hi, z).
Axes of the slice: x: 4, y: 4 (y_hi: 2, y_lo: 2; y = y_hi * 2 + y_lo), z: 4, core: 2. Of those that a mesh axis runs over, the one named last changes fastest.
Arguments:
- tokens: bfloat16 [32768, 1024], P(('dp', 'fsdp')), may hold values from -24 to 24
- positions: int32 [32768], P(('dp', 'fsdp')), may hold values from 0 to 255, as said below
- w_query: bfloat16 [1024, 2048], P('dp', 'fsdp'), may hold values from -0.1875 to 0.1875
- w_key: bfloat16 [1024, 1024], P('dp', 'fsdp'), may hold values from -0.1875 to 0.1875
- w_value: bfloat16 [1024, 1024], P('dp', 'fsdp'), may hold values from -0.1875 to 0.1875
- w_out: bfloat16 [2048, 1024], P('fsdp', 'dp'), may hold values from -0.125 to 0.125
- w_gate: bfloat16 [1024, 3072], P('dp', 'fsdp'), may hold values from -0.1875 to 0.1875
- w_up: bfloat16 [1024, 3072], P('dp', 'fsdp'), may hold values from -0.1875 to 0.1875
- w_down: bfloat16 [3072, 1024], P('fsdp', 'dp'), may hold values from -0.109375 to 0.109375
- query_gain: bfloat16 [128], P('dp'), may hold values from 1 to 2
- key_gain: bfloat16 [128], P('dp'), may hold values from 1 to 2
- attn_gain: bfloat16 [1024], P('dp'), may hold values from 0.5 to 2
- ffn_gain: bfloat16 [1024], P('dp'), may hold values from 0.5 to 2
- cotangent: bfloat16 [32768, 1024], P(('dp', 'fsdp')), may hold values from -24 to 24
Outputs:
- mixed: bfloat16 [32768, 1024], P(('dp', 'fsdp'))
- tokens_grad: float32 [32768, 1024], P(('dp', 'fsdp'))
- w_query_grad: float32 [1024, 2048], P('dp', 'fsdp')
- w_key_grad: float32 [1024, 1024], P('dp', 'fsdp')
- w_value_grad: float32 [1024, 1024], P('dp', 'fsdp')
- w_out_grad: float32 [2048, 1024], P('fsdp', 'dp')
- w_gate_grad: float32 [1024, 3072], P('dp', 'fsdp')
- w_up_grad: float32 [1024, 3072], P('dp', 'fsdp')
- w_down_grad: float32 [3072, 1024], P('fsdp', 'dp')
- query_gain_grad: float32 [128], P('dp')
- key_gain_grad: float32 [128], P('dp')
- attn_gain_grad: float32 [1024], P('dp')
- ffn_gain_grad: float32 [1024], P('dp')
Inputs may be any that keep to these rules, and one draw needn't show every extreme that they name: Every aligned block of 256 tokens holds whole sequences: each sequence's positions run 0, 1, 2, ... in consecutive slots, and every block begins with 0. In every draw one block holds a single sequence of 256 tokens.
All inputs are finite; a program needn't handle non-finite values.
Results may differ from a plain program's by a relative error of at most 0.025.
Values may be sent and summed in bfloat16 or wider, within the bound.
A program may use at most 192 MiB of HBM per device.

v0:
```python
import jax
import jax.numpy as jnp
from jax import lax
from jax.sharding import PartitionSpec as P

HD = 128
TOK_DEV = 256


EPS = 1e-06
ROPE_BASE = 1000000.0


def rope_tables(places, head_width):
    steps_up = jnp.arange(0, head_width, 2).astype(jnp.float32) / head_width
    inverse = ROPE_BASE ** (-steps_up)
    angles = places.astype(jnp.float32)[:, None] * inverse[None, :]
    cosine = jnp.cos(angles)
    sine_part = jnp.sin(angles)
    return (jnp.concatenate([cosine, cosine], -1), jnp.concatenate([sine_part, sine_part], -1))


def rms_scale(values_in, gain_in):
    return (
        values_in
        * lax.rsqrt(jnp.mean(values_in * values_in, axis=-1, keepdims=True) + EPS)
        * gain_in
    )


def rotate(values_in, cosine, sine_part):
    half_size = values_in.shape[-1] // 2
    turned = jnp.concatenate([-values_in[..., half_size:], values_in[..., :half_size]], -1)
    return values_in * cosine + turned * sine_part


def prepare(raw, gain_in, cosine, sine_part):
    head_count = raw.shape[1] // HD
    shaped = raw.reshape(raw.shape[0], head_count, HD)
    return rotate(rms_scale(shaped, gain_in), cosine[:, None, :], sine_part[:, None, :])


def fetch_weights(
    w_query, w_key, w_value, w_out, w_gate, w_up, w_down, query_gain, key_gain, attn_gain, ffn_gain
):
    fetched = (
        lax.all_gather(w_query, "dp", axis=0, tiled=True),
        lax.all_gather(w_key, "dp", axis=0, tiled=True),
        lax.all_gather(w_value, "dp", axis=0, tiled=True),
        lax.all_gather(w_out, "dp", axis=1, tiled=True),
        lax.all_gather(w_gate, "dp", axis=0, tiled=True),
        lax.all_gather(w_up, "dp", axis=0, tiled=True),
        lax.all_gather(w_down, "dp", axis=1, tiled=True),
        lax.all_gather(query_gain, "dp", axis=0, tiled=True),
        lax.all_gather(key_gain, "dp", axis=0, tiled=True),
        lax.all_gather(attn_gain, "dp", axis=0, tiled=True),
        lax.all_gather(ffn_gain, "dp", axis=0, tiled=True),
    )
    whole = (
        lax.all_gather(fetched[0], "fsdp", axis=1, tiled=True),
        lax.all_gather(fetched[1], "fsdp", axis=1, tiled=True),
        lax.all_gather(fetched[2], "fsdp", axis=1, tiled=True),
        lax.all_gather(fetched[3], "fsdp", axis=0, tiled=True),
        lax.all_gather(fetched[4], "fsdp", axis=1, tiled=True),
        lax.all_gather(fetched[5], "fsdp", axis=1, tiled=True),
        lax.all_gather(fetched[6], "fsdp", axis=0, tiled=True),
    )
    return (tuple(whole), fetched[7:])


def on_device(
    tokens,
    positions,
    w_query,
    w_key,
    w_value,
    w_out,
    w_gate,
    w_up,
    w_down,
    query_gain,
    key_gain,
    attn_gain,
    ffn_gain,
    cotangent,
):
    shards = (
        w_query,
        w_key,
        w_value,
        w_out,
        w_gate,
        w_up,
        w_down,
        query_gain,
        key_gain,
        attn_gain,
        ffn_gain,
    )
    mats, gains = fetch_weights(*shards)
    query_full, key_full, value_full, out_full, gate_full, up_full, down_full = mats
    qgain_wide = gains[0].astype(jnp.float32)
    kgain_wide = gains[1].astype(jnp.float32)
    again_wide = gains[2].astype(jnp.float32)
    fgain_wide = gains[3].astype(jnp.float32)
    group_tokens, places = (tokens, positions)
    row_count = group_tokens.shape[0]
    head_count = query_full.shape[1] // HD
    kv_count = key_full.shape[1] // HD
    group_size = head_count // kv_count
    block_size = min(512, row_count)
    window_size = max(block_size, TOK_DEV)
    starts = jnp.arange(row_count // block_size, dtype=jnp.int32) * block_size
    scale = HD ** (-0.5)
    cosine, sine_part = rope_tables(places, HD)
    inputs = tokens.astype(jnp.float32)
    q_raw = jnp.dot(group_tokens, query_full, preferred_element_type=jnp.float32)
    k_raw = jnp.dot(group_tokens, key_full, preferred_element_type=jnp.float32)
    v_raw = jnp.dot(group_tokens, value_full, preferred_element_type=jnp.float32)
    query_low = (
        prepare(q_raw, qgain_wide, cosine, sine_part)
        .astype(jnp.bfloat16)
        .reshape(row_count, kv_count, group_size, HD)
    )
    keys_low = prepare(k_raw, kgain_wide, cosine, sine_part).astype(jnp.bfloat16)
    values_low = v_raw.astype(jnp.bfloat16).reshape(row_count, kv_count, HD)

    def block_scores(start, query_block):
        first_key = start // window_size * window_size
        query_slots = start + jnp.arange(block_size, dtype=jnp.int32)
        key_slots = first_key + jnp.arange(window_size, dtype=jnp.int32)
        earliest = query_slots - places
        allowed = (key_slots[None, :] <= query_slots[:, None]) & (
            key_slots[None, :] >= earliest[:, None]
        )
        scores = (
            jnp.einsum("qgrd,kgd->grqk", query_block, keys_low, preferred_element_type=jnp.float32)
            * scale
        )
        return (jnp.where(allowed[None, None], scores, -1e30), first_key, keys_low)

    def attend(start):
        scores, first_key, keys_window = block_scores(start, query_low)
        row_top = jnp.max(scores, axis=-1, keepdims=True)
        weights = jnp.exp(scores - row_top)
        row_total = jnp.sum(weights, axis=-1, keepdims=True)
        probs_low = (weights / row_total).astype(jnp.bfloat16)
        result = jnp.einsum(
            "grqk,kgd->qgrd", probs_low, values_low, preferred_element_type=jnp.float32
        )
        return (result.reshape(block_size, -1).astype(jnp.bfloat16), row_top + jnp.log(row_total))

    attended, log_totals = lax.map(attend, starts)
    attended = attended.reshape(row_count, head_count * HD)
    branch = jnp.dot(attended, out_full, preferred_element_type=jnp.float32)
    hidden = inputs + rms_scale(branch, again_wide)
    hidden_low = hidden.astype(jnp.bfloat16)
    gate = jnp.dot(hidden_low, gate_full, preferred_element_type=jnp.float32)
    upward = jnp.dot(hidden_low, up_full, preferred_element_type=jnp.float32)
    act_low = (jax.nn.silu(gate) * upward).astype(jnp.bfloat16)
    ffn = jnp.dot(act_low, down_full, preferred_element_type=jnp.float32)
    mixed = (hidden + rms_scale(ffn, fgain_wide)).astype(jnp.bfloat16)
    back_mats, unused_gains = fetch_weights(*shards)
    query_back, key_back, value_back, out_back, gate_back, up_back, down_back = back_mats
    out_grad = cotangent.astype(jnp.float32)
    ffn_pull = jax.vjp(rms_scale, ffn, fgain_wide)[1]
    ffn_grad, fgain_grad = ffn_pull(out_grad)
    group_ffn_grad = ffn_grad.astype(jnp.bfloat16)
    down_wgrad = jnp.einsum(
        "tf,td->fd", act_low, group_ffn_grad, preferred_element_type=jnp.float32
    )
    act_grad = jnp.einsum(
        "td,fd->tf", group_ffn_grad, down_back, preferred_element_type=jnp.float32
    )
    swish_pull = jax.vjp(lambda gate_in, up_in: jax.nn.silu(gate_in) * up_in, gate, upward)[1]
    gate_grad, up_grad = swish_pull(act_grad)
    gate_grad_low = gate_grad.astype(jnp.bfloat16)
    up_grad_low = up_grad.astype(jnp.bfloat16)
    gate_wgrad = jnp.einsum(
        "td,tf->df", hidden_low, gate_grad_low, preferred_element_type=jnp.float32
    )
    up_wgrad = jnp.einsum("td,tf->df", hidden_low, up_grad_low, preferred_element_type=jnp.float32)
    hidden_part = jnp.einsum(
        "tf,df->td", gate_grad_low, gate_back, preferred_element_type=jnp.float32
    )
    hidden_part = hidden_part + jnp.einsum(
        "tf,df->td", up_grad_low, up_back, preferred_element_type=jnp.float32
    )
    hidden_grad = out_grad + hidden_part
    branch_pull = jax.vjp(rms_scale, branch, again_wide)[1]
    branch_grad, again_grad = branch_pull(hidden_grad)
    group_branch_grad = branch_grad.astype(jnp.bfloat16)
    out_wgrad = jnp.einsum(
        "tq,td->qd", attended, group_branch_grad, preferred_element_type=jnp.float32
    )
    attended_grad_low = jnp.einsum(
        "td,qd->tq", group_branch_grad, out_back, preferred_element_type=jnp.float32
    ).astype(jnp.bfloat16)
    attended_grad_low = attended_grad_low.reshape(row_count, kv_count, group_size, HD)

    def attend_back(carry, item):
        key_grad, value_grad = carry
        start, log_block = item
        scores, first_key, keys_window = block_scores(start, query_low)
        probs = jnp.exp(scores - log_block)
        probs_low = probs.astype(jnp.bfloat16)
        value_part = jnp.einsum(
            "grqk,qgrd->kgd", probs_low, attended_grad_low, preferred_element_type=jnp.float32
        )
        prob_grad = jnp.einsum(
            "qgrd,kgd->grqk", attended_grad_low, values_low, preferred_element_type=jnp.float32
        )
        score_grad_low = (
            probs * (prob_grad - jnp.sum(probs * prob_grad, axis=-1, keepdims=True))
        ).astype(jnp.bfloat16)
        query_grad = (
            jnp.einsum(
                "grqk,kgd->qgrd", score_grad_low, keys_window, preferred_element_type=jnp.float32
            )
            * scale
        )
        key_part = (
            jnp.einsum(
                "grqk,qgrd->kgd", score_grad_low, query_low, preferred_element_type=jnp.float32
            )
            * scale
        )
        value_grad = value_grad + value_part
        key_grad = key_grad + key_part
        return ((key_grad, value_grad), query_grad.reshape(block_size, -1))

    zeroed = jnp.zeros((row_count, kv_count, HD), jnp.float32)
    (key_grad, value_grad), query_grad = lax.scan(
        attend_back, (zeroed, zeroed), (starts, log_totals)
    )
    query_grad = query_grad.reshape(row_count, head_count, HD)
    query_pull = jax.vjp(
        lambda raw, gain_in: prepare(raw, gain_in, cosine, sine_part), q_raw, qgain_wide
    )[1]
    q_raw_grad, qgain_grad = query_pull(query_grad)
    key_pull = jax.vjp(
        lambda raw, gain_in: prepare(raw, gain_in, cosine, sine_part), k_raw, kgain_wide
    )[1]
    k_raw_grad, kgain_grad = key_pull(key_grad)
    q_grad_low = q_raw_grad.astype(jnp.bfloat16)
    k_grad_low = k_raw_grad.astype(jnp.bfloat16)
    v_grad_low = value_grad.reshape(row_count, -1).astype(jnp.bfloat16)
    query_wgrad = jnp.einsum(
        "td,tq->dq", group_tokens, q_grad_low, preferred_element_type=jnp.float32
    )
    key_wgrad = jnp.einsum(
        "td,tq->dq", group_tokens, k_grad_low, preferred_element_type=jnp.float32
    )
    value_wgrad = jnp.einsum(
        "td,tq->dq", group_tokens, v_grad_low, preferred_element_type=jnp.float32
    )
    input_part = jnp.einsum("tq,dq->td", q_grad_low, query_back, preferred_element_type=jnp.float32)
    input_part = input_part + jnp.einsum(
        "tq,dq->td", k_grad_low, key_back, preferred_element_type=jnp.float32
    )
    input_part = input_part + jnp.einsum(
        "tq,dq->td", v_grad_low, value_back, preferred_element_type=jnp.float32
    )
    tokens_grad = hidden_grad + input_part
    qgain_all, kgain_all, again_all, fgain_all = lax.psum(
        (qgain_grad, kgain_grad, again_grad, fgain_grad), "fsdp"
    )
    query_wgrad, key_wgrad, value_wgrad, out_wgrad, gate_wgrad, up_wgrad, down_wgrad = (
        lax.psum_scatter(
            query_wgrad.astype(jnp.bfloat16), "fsdp", scatter_dimension=1, tiled=True
        ).astype(jnp.float32),
        lax.psum_scatter(
            key_wgrad.astype(jnp.bfloat16), "fsdp", scatter_dimension=1, tiled=True
        ).astype(jnp.float32),
        lax.psum_scatter(
            value_wgrad.astype(jnp.bfloat16), "fsdp", scatter_dimension=1, tiled=True
        ).astype(jnp.float32),
        lax.psum_scatter(
            out_wgrad.astype(jnp.bfloat16), "fsdp", scatter_dimension=0, tiled=True
        ).astype(jnp.float32),
        lax.psum_scatter(
            gate_wgrad.astype(jnp.bfloat16), "fsdp", scatter_dimension=1, tiled=True
        ).astype(jnp.float32),
        lax.psum_scatter(
            up_wgrad.astype(jnp.bfloat16), "fsdp", scatter_dimension=1, tiled=True
        ).astype(jnp.float32),
        lax.psum_scatter(
            down_wgrad.astype(jnp.bfloat16), "fsdp", scatter_dimension=0, tiled=True
        ).astype(jnp.float32),
    )
    summed = (
        lax.psum_scatter(
            query_wgrad.astype(jnp.bfloat16), "dp", scatter_dimension=0, tiled=True
        ).astype(jnp.float32),
        lax.psum_scatter(
            key_wgrad.astype(jnp.bfloat16), "dp", scatter_dimension=0, tiled=True
        ).astype(jnp.float32),
        lax.psum_scatter(
            value_wgrad.astype(jnp.bfloat16), "dp", scatter_dimension=0, tiled=True
        ).astype(jnp.float32),
        lax.psum_scatter(
            out_wgrad.astype(jnp.bfloat16), "dp", scatter_dimension=1, tiled=True
        ).astype(jnp.float32),
        lax.psum_scatter(
            gate_wgrad.astype(jnp.bfloat16), "dp", scatter_dimension=0, tiled=True
        ).astype(jnp.float32),
        lax.psum_scatter(
            up_wgrad.astype(jnp.bfloat16), "dp", scatter_dimension=0, tiled=True
        ).astype(jnp.float32),
        lax.psum_scatter(
            down_wgrad.astype(jnp.bfloat16), "dp", scatter_dimension=1, tiled=True
        ).astype(jnp.float32),
        lax.psum_scatter(
            qgain_all.astype(jnp.bfloat16), "dp", scatter_dimension=0, tiled=True
        ).astype(jnp.float32),
        lax.psum_scatter(
            kgain_all.astype(jnp.bfloat16), "dp", scatter_dimension=0, tiled=True
        ).astype(jnp.float32),
        lax.psum_scatter(
            again_all.astype(jnp.bfloat16), "dp", scatter_dimension=0, tiled=True
        ).astype(jnp.float32),
        lax.psum_scatter(
            fgain_all.astype(jnp.bfloat16), "dp", scatter_dimension=0, tiled=True
        ).astype(jnp.float32),
    )
    return (
        mixed,
        tokens_grad,
        summed[0],
        summed[1],
        summed[2],
        summed[3],
        summed[4],
        summed[5],
        summed[6],
        summed[7],
        summed[8],
        summed[9],
        summed[10],
    )


def solution(mesh):
    placed = (
        P(("dp", "fsdp"), None),
        P(("dp", "fsdp")),
        P("dp", "fsdp"),
        P("dp", "fsdp"),
        P("dp", "fsdp"),
        P("fsdp", "dp"),
        P("dp", "fsdp"),
        P("dp", "fsdp"),
        P("fsdp", "dp"),
        P("dp"),
        P("dp"),
        P("dp"),
        P("dp"),
        P(("dp", "fsdp"), None),
    )
    return jax.shard_map(
        on_device,
        mesh=mesh,
        in_specs=placed,
        out_specs=(
            P(("dp", "fsdp"), None),
            P(("dp", "fsdp"), None),
            P("dp", "fsdp"),
            P("dp", "fsdp"),
            P("dp", "fsdp"),
            P("fsdp", "dp"),
            P("dp", "fsdp"),
            P("dp", "fsdp"),
            P("fsdp", "dp"),
            P("dp"),
            P("dp"),
            P("dp"),
            P("dp"),
        ),
        check_vma=False,
    )
```

profile of v0, /device:TPU:1, one launch (start us, length us, event | category | flops | bytes accessed | tf_op | source)
XLA Modules:
  0.0 1664.7 jit_solution(4311608394188348844)
XLA Ops:
  7.2 23.4 %all_gather.68 = bf16[1024,128]{1,0:T(8,128)(2,1)} all-gather(bf16[64,128]{1,0:T(8,128)(2,1)} %param.18), channel_id=1, replica_groups=mesh['dp'=16,'fsdp'=8] {'dp'}, dimensions={0}, use_global_device_ids=true | all-gather | bytes 278528 | tf_op jit(solution)/shard_map/all_gather | solution.py:49
  30.7 18.7 %all_gather.70 = bf16[1024,128]{1,0:T(8,128)(2,1)} all-gather(bf16[64,128]{1,0:T(8,128)(2,1)} %param.17), channel_id=1, replica_groups=mesh['dp'=16,'fsdp'=8] {'dp'}, dimensions={0}, use_global_device_ids=true | all-gather | bytes 278528 | tf_op jit(solution)/shard_map/all_gather | solution.py:48
  49.5 20.7 %all_gather.73 = bf16[1024,256]{1,0:T(8,128)(2,1)} all-gather(bf16[64,256]{1,0:T(8,128)(2,1)} %param.16), channel_id=1, replica_groups=mesh['dp'=16,'fsdp'=8] {'dp'}, dimensions={0}, use_global_device_ids=true | all-gather | bytes 557056 | tf_op jit(solution)/shard_map/all_gather | solution.py:47
  70.3 19.3 %all_gather.76 = bf16[256,1024]{0,1:T(8,128)(2,1)} all-gather(bf16[256,64]{0,1:T(8,128)(2,1)} %param.19), channel_id=1, replica_groups=mesh['dp'=16,'fsdp'=8] {'dp'}, dimensions={1}, use_global_device_ids=true | all-gather | bytes 557056 | tf_op jit(solution)/shard_map/all_gather | solution.py:50
  89.8 21.3 %all_gather.79 = bf16[1024,384]{1,0:T(8,128)(2,1)} all-gather(bf16[64,384]{1,0:T(8,128)(2,1)S(1)} %copy-done.52), channel_id=1, replica_groups=mesh['dp'=16,'fsdp'=8] {'dp'}, dimensions={0}, use_global_device_ids=true | all-gather | bytes 835584 | tf_op jit(solution)/shard_map/all_gather | solution.py:51
  111.2 20.1 %all_gather.81 = bf16[1024,384]{1,0:T(8,128)(2,1)} all-gather(bf16[64,384]{1,0:T(8,128)(2,1)S(1)} %copy-done.53), channel_id=1, replica_groups=mesh['dp'=16,'fsdp'=8] {'dp'}, dimensions={0}, use_global_device_ids=true | all-gather | bytes 835584 | tf_op jit(solution)/shard_map/all_gather | solution.py:52
  131.4 21.1 %all_gather.83 = bf16[384,1024]{0,1:T(8,128)(2,1)} all-gather(bf16[384,64]{0,1:T(8,128)(2,1)S(1)} %copy-done.54), channel_id=1, replica_groups=mesh['dp'=16,'fsdp'=8] {'dp'}, dimensions={1}, use_global_device_ids=true | all-gather | bytes 835584 | tf_op jit(solution)/shard_map/all_gather | solution.py:53
  155.4 27.6 %all-reduce.14 = (bf16[128]{0:T(256)(128)(2,1)S(1)}, bf16[128]{0:T(256)(128)(2,1)S(1)}, bf16[1024]{0:T(1024)(128)(2,1)S(1)}, bf16[1024]{0:T(1024)(128)(2,1)S(1)}) all-reduce(bf16[128]{0:T(256)(128)(2,1)S(1)} %dynamic-update-slice, bf16[128]{0:T(256)(128)(2,1)S(1)} %dynamic-update-slice.1, ...), channel_id=1, replica_groups=mesh['dp'=16,'fsdp'=8] {'dp'}, use_global_device_ids=true, to_apply=%add.4 | all-reduce | flops 2304 | bytes 9216
  186.4 2.3 fusion.28
  189.6 2.3 convolution_bitcast_fusion
  194.7 20.8 %all-gather.12.cloned.1.call-done = bf16[1024,2048]{1,0:T(8,128)(2,1)} async-done(((bf16[1024,256]{1,0:T(8,128)(2,1)}), bf16[1024,2048]{1,0:T(8,128)(2,1)}) %all-gather.12.cloned.1.call-update) | async-done | bytes 4194320 | tf_op jit(solution)/shard_map/all_gather | solution.py:60
  215.6 4.1 multiply_reduce_fusion.2
  226.2 1.9 fusion.18
  228.0 60.9 %all-gather.14.cloned.1.call-done = bf16[2048,1024]{0,1:T(8,128)(2,1)} async-done(((bf16[256,1024]{0,1:T(8,128)(2,1)}), bf16[2048,1024]{0,1:T(8,128)(2,1)}) %all-gather.14.cloned.1.call-update) | async-done | bytes 4194320 | tf_op jit(solution)/shard_map/all_gather | solution.py:63
  288.9 3.9 multiply_reduce_fusion.8
  295.0 87.4 %all-gather.16.cloned.1.call-done = bf16[1024,3072]{1,0:T(8,128)(2,1)} async-done(((bf16[1024,384]{1,0:T(8,128)(2,1)}), bf16[1024,3072]{1,0:T(8,128)(2,1)}) %all-gather.16.cloned.1.call-update) | async-done | bytes 6291472 | tf_op jit(solution)/shard_map/all_gather | solution.py:64
  382.4 6.5 fusion.53
  388.9 87.0 %all-gather.18.cloned.1.call-done = bf16[1024,3072]{1,0:T(8,128)(2,1)} async-done(((bf16[1024,384]{1,0:T(8,128)(2,1)}), bf16[1024,3072]{1,0:T(8,128)(2,1)}) %all-gather.18.cloned.1.call-update) | async-done | bytes 6291472 | tf_op jit(solution)/shard_map/all_gather | solution.py:65
  475.9 8.3 multiply_convert_fusion.1
  484.2 85.3 %all-gather.20.cloned.1.call-done = bf16[3072,1024]{0,1:T(8,128)(2,1)} async-done(((bf16[384,1024]{0,1:T(8,128)(2,1)}), bf16[3072,1024]{0,1:T(8,128)(2,1)}) %all-gather.20.cloned.1.call-update) | async-done | bytes 6291472 | tf_op jit(solution)/shard_map/all_gather | solution.py:66
  569.5 5.3 multiply_reduce_fusion.7
  575.9 6.4 multiply_convert_fusion
  582.4 1.8 fusion.54
  584.4 2.8 multiply_reduce_fusion.3
  590.2 2.3 convolution_convert_fusion.4
  592.4 2.4 copy.164
  594.9 3.4 fusion.23
  599.1 2.0 convert_bitcast_fusion.1
  601.2 3.7 fusion
  609.5 2.1 convert_bitcast_fusion.2
  611.7 2.0 convolution_multiply_fusion
  616.8 3.3 convert_bitcast_fusion
  621.5 3.2 convolution_convert_fusion.3
  626.0 6.1 convolution_convert_fusion
  633.7 4.4 convolution_convert_fusion.1
  638.1 8.7 copy.160
  648.2 4.5 convolution_convert_fusion.2
  652.7 8.7 copy.158
  661.6 11.7 reduce-scatter.33.cloned.1.call-done
  673.3 1.8 copy.154
  675.1 75.7 %reduce-scatter.31.cloned.1.call-done = bf16[1024,128]{0,1:T(8,128)(2,1)} async-done(((bf16[1024,1024]{0,1:T(8,128)(2,1)}), bf16[1024,128]{0,1:T(8,128)(2,1)}) %reduce-scatter.31.cloned.1.call-update) | async-done | bytes 262160 | tf_op jit(solution)/shard_map/reduce_scatter | solution.py:272
  750.8 1.8 copy.152
  752.7 85.6 %reduce-scatter.29.cloned.1.call-done = bf16[1024,256]{0,1:T(8,128)(2,1)} async-done(((bf16[1024,2048]{0,1:T(8,128)(2,1)}), bf16[1024,256]{0,1:T(8,128)(2,1)}) %reduce-scatter.29.cloned.1.call-update) | async-done | bytes 524304 | tf_op jit(solution)/shard_map/reduce_scatter | solution.py:269
  838.3 2.0 copy.150
  840.4 85.7 %reduce-scatter.35.cloned.1.call-done = bf16[256,1024]{1,0:T(8,128)(2,1)} async-done(((bf16[2048,1024]{1,0:T(8,128)(2,1)}), bf16[256,1024]{1,0:T(8,128)(2,1)}) %reduce-scatter.35.cloned.1.call-update) | async-done | bytes 524304 | tf_op jit(solution)/shard_map/reduce_scatter | solution.py:278
  926.1 2.0 copy.156
  928.2 99.4 %reduce-scatter.41.cloned.1.call-done = bf16[384,1024]{1,0:T(8,128)(2,1)} async-done(((bf16[3072,1024]{1,0:T(8,128)(2,1)}), bf16[384,1024]{1,0:T(8,128)(2,1)}) %reduce-scatter.41.cloned.1.call-update) | async-done | bytes 786448 | tf_op jit(solution)/shard_map/reduce_scatter | solution.py:287
  1027.6 2.3 copy.162
  1030.0 98.4 %reduce-scatter.53.cloned.1.call-done = bf16[384,1024]{1,0:T(8,128)(2,1)} async-done(((bf16[3072,1024]{1,0:T(8,128)(2,1)}), bf16[384,1024]{1,0:T(8,128)(2,1)}) %reduce-scatter.53.cloned.1.call-update) | async-done | bytes 786448
  1128.3 2.3 copy.161
  1130.7 98.2 %reduce-scatter.51.cloned.1.call-done = bf16[384,1024]{1,0:T(8,128)(2,1)} async-done(((bf16[3072,1024]{1,0:T(8,128)(2,1)}), bf16[384,1024]{1,0:T(8,128)(2,1)}) %reduce-scatter.51.cloned.1.call-update) | async-done | bytes 786448
  1228.9 2.3 copy.159
  1232.5 30.5 %all-reduce.12 = (bf16[128]{0:T(256)(128)(2,1)S(1)}, bf16[128]{0:T(256)(128)(2,1)S(1)}, bf16[1024]{0:T(1024)(128)(2,1)S(1)}, bf16[1024]{0:T(1024)(128)(2,1)S(1)}) all-reduce(f32[128]{0:T(128)S(1)} %get-tuple-element.120, f32[128]{0:T(128)S(1)} %copy-done.71, f32[1024]{0:T(1024)S(1)} %copy-done.70, ...), channel_id=1, replica_groups=mesh['dp'=16,'fsdp'=8] {'fsdp'}, use_global_device_ids=true, to_apply=%region_26.27 | all-reduce | flops 2304 | bytes 13824 | tf_op jit(solution)/shard_map/psum | solution.py:265
  1263.0 36.2 %all-reduce.13 = (bf16[128]{0:T(256)(128)(2,1)S(1)}, bf16[128]{0:T(256)(128)(2,1)S(1)}, bf16[1024]{0:T(1024)(128)(2,1)S(1)}, bf16[1024]{0:T(1024)(128)(2,1)S(1)}) all-reduce(bf16[128]{0:T(256)(128)(2,1)S(1)} %get-tuple-element.124, bf16[128]{0:T(256)(128)(2,1)S(1)} %get-tuple-element.125, ...), channel_id=16, replica_groups=mesh['dp'=16,'fsdp'=8] {'dp'}, use_global_device_ids=true, to_apply=%region_27.28.clone | all-reduce | flops 2304 | bytes 9216
  1300.4 3.6 fusion.55
  1306.1 1.7 fusion.22
  1309.4 38.3 %reduce-scatter.45.cloned.1.call-done = bf16[64,128]{1,0:T(8,128)(2,1)} async-done(((bf16[1024,128]{1,0:T(8,128)(2,1)}), bf16[64,128]{1,0:T(8,128)(2,1)}) %reduce-scatter.45.cloned.1.call-update) | async-done | bytes 16400
  1349.3 59.6 %reduce-scatter.43.cloned.1.call-done = bf16[64,256]{1,0:T(8,128)(2,1)} async-done(((bf16[1024,256]{1,0:T(8,128)(2,1)}), bf16[64,256]{1,0:T(8,128)(2,1)}) %reduce-scatter.43.cloned.1.call-update) | async-done | bytes 32784
  1410.5 59.8 %reduce-scatter.49.cloned.1.call-done = bf16[64,256]{1,0:T(8,128)(2,1)} async-done(((bf16[1024,256]{1,0:T(8,128)(2,1)}), bf16[64,256]{1,0:T(8,128)(2,1)}) %reduce-scatter.49.cloned.1.call-update) | async-done | bytes 32784
  1472.0 60.4 %reduce-scatter.55.cloned.1.call-done = bf16[64,384]{1,0:T(8,128)(2,1)} async-done(((bf16[1024,384]{1,0:T(8,128)(2,1)}), bf16[64,384]{1,0:T(8,128)(2,1)}) %reduce-scatter.55.cloned.1.call-update) | async-done | bytes 49168
  1534.0 60.1 %reduce-scatter.39.cloned.1.call-done = bf16[64,384]{1,0:T(8,128)(2,1)} async-done(((bf16[1024,384]{1,0:T(8,128)(2,1)}), bf16[64,384]{1,0:T(8,128)(2,1)}) %reduce-scatter.39.cloned.1.call-update) | async-done | bytes 49168 | tf_op jit(solution)/shard_map/reduce_scatter | solution.py:307
  1594.1 1.4 convert_element_type.240
  1595.6 60.4 %reduce-scatter.37.cloned.1.call-done = bf16[64,384]{1,0:T(8,128)(2,1)} async-done(((bf16[1024,384]{1,0:T(8,128)(2,1)}), bf16[64,384]{1,0:T(8,128)(2,1)}) %reduce-scatter.37.cloned.1.call-update) | async-done | bytes 49168 | tf_op jit(solution)/shard_map/reduce_scatter | solution.py:304
  1655.9 1.4 convert_element_type.238
  (284 shorter events, 47.1 us)
Async XLA Ops:
  7.2 82.6 %copy-start.52 = (bf16[64,384]{1,0:T(8,128)(2,1)S(1)}, bf16[64,384]{1,0:T(8,128)(2,1)}, u32[]{:S(2)}) copy-start(bf16[64,384]{1,0:T(8,128)(2,1)} %param.20) | copy-start | bytes 147460
  7.2 104.0 %copy-start.53 = (bf16[64,384]{1,0:T(8,128)(2,1)S(1)}, bf16[64,384]{1,0:T(8,128)(2,1)}, u32[]{:S(2)}) copy-start(bf16[64,384]{1,0:T(8,128)(2,1)} %param.21) | copy-start | bytes 147460
  7.2 179.2 %all-gather.8.cloned.1.call-start = ((), (), s32[]{:S(2)}) async-start(), calls=%async_computation.14 | async-start | bytes 2359296 | tf_op jit(solution)/shard_map/all_gather | solution.py:62
  30.6 100.7 %copy-start.54 = (bf16[384,64]{0,1:T(8,128)(2,1)S(1)}, bf16[384,64]{0,1:T(8,128)(2,1)}, u32[]{:S(2)}) copy-start(bf16[384,64]{0,1:T(8,128)(2,1)} %param.22) | copy-start | bytes 147460
  30.7 159.0 %all-gather.10.cloned.1.call-start = ((), (), s32[]{:S(2)}) async-start(), calls=%async_computation.15 | async-start | bytes 2359296 | tf_op jit(solution)/shard_map/all_gather | solution.py:61
  49.4 166.1 %all-gather.12.cloned.1.call-start = ((), (), s32[]{:S(2)}) async-start(), calls=%async_computation.16 | async-start | bytes 4718592 | tf_op jit(solution)/shard_map/all_gather | solution.py:60
  70.2 82.3 %copy-start.72 = (u32[128]{0:T(128)S(1)}, u32[128]{0:T(128)}, u32[]{:S(2)}) copy-start(u32[128]{0:T(128)} %constant.126) | copy-start | bytes 1540
  70.2 84.2 %copy-start.76 = (bf16[8]{0:T(256)(128)(2,1)S(1)}, bf16[8]{0:T(256)(128)(2,1)}, u32[]{:S(2)}) copy-start(bf16[8]{0:T(256)(128)(2,1)} %param.24) | copy-start | bytes 52
  70.2 84.5 %copy-start.77 = (bf16[8]{0:T(256)(128)(2,1)S(1)}, bf16[8]{0:T(256)(128)(2,1)}, u32[]{:S(2)}) copy-start(bf16[8]{0:T(256)(128)(2,1)} %param.23) | copy-start | bytes 52
  70.2 84.7 %copy-start.78 = (bf16[64]{0:T(256)(128)(2,1)S(1)}, bf16[64]{0:T(256)(128)(2,1)}, u32[]{:S(2)}) copy-start(bf16[64]{0:T(256)(128)(2,1)} %param.25) | copy-start | bytes 388
  70.2 85.0 %copy-start.79 = (bf16[64]{0:T(256)(128)(2,1)S(1)}, bf16[64]{0:T(256)(128)(2,1)}, u32[]{:S(2)}) copy-start(bf16[64]{0:T(256)(128)(2,1)} %param.26) | copy-start | bytes 388
  70.3 114.5 %copy-start.73 = (s32[256]{0:T(256)S(1)}, s32[256]{0:T(256)}, u32[]{:S(2)}) copy-start(s32[256]{0:T(256)} %param.15) | copy-start | bytes 3076
  70.3 218.6 %all-gather.14.cloned.1.call-start = ((), (), s32[]{:S(2)}) async-start(), calls=%async_computation.17 | async-start | bytes 4718592 | tf_op jit(solution)/shard_map/all_gather | solution.py:63
  89.7 96.7 %copy-start.3 = (bf16[256,1024]{1,0:T(8,128)(2,1)S(1)}, bf16[256,1024]{1,0:T(8,128)(2,1)}, u32[]{:S(2)}) copy-start(bf16[256,1024]{1,0:T(8,128)(2,1)} %param.14) | copy-start | bytes 1572868
  89.7 292.7 %all-gather.16.cloned.1.call-start = ((), (), s32[]{:S(2)}) async-start(), calls=%async_computation.18 | async-start | bytes 7077888 | tf_op jit(solution)/shard_map/all_gather | solution.py:64
  111.1 364.7 %all-gather.18.cloned.1.call-start = ((), (), s32[]{:S(2)}) async-start(), calls=%async_computation.19 | async-start | bytes 7077888 | tf_op jit(solution)/shard_map/all_gather | solution.py:65
  131.3 438.2 %all-gather.20.cloned.1.call-start = ((), (), s32[]{:S(2)}) async-start(), calls=%async_computation.20 | async-start | bytes 7077888 | tf_op jit(solution)/shard_map/all_gather | solution.py:66
  152.5 520.8 %reduce-scatter.33.cloned.1.call-start = ((), (), s32[]{:S(2)}) async-start(), calls=%async_computation.23 | async-start | bytes 2359296 | tf_op jit(solution)/shard_map/reduce_scatter | solution.py:275
  183.0 10.3 copy-start.62
  288.9 4.0 copy-start.42
  288.9 4.0 copy-start.48
  288.9 5.0 copy-start.4
  288.9 5.0 copy-start.55
  569.5 5.4 copy-start.28
  569.5 5.4 copy-start.45
  569.5 6.4 copy-start.74
  569.5 6.4 copy-start.80
  574.8 12.5 copy-start.9
  574.8 12.5 copy-start.57
  574.8 7.5 slice-start
  574.8 9.4 slice-start.2
  575.8 6.5 copy-start.66
  575.9 6.5 slice-start.1
  575.9 8.4 slice-start.3
  582.4 2.0 copy-start.22
  582.4 2.0 copy-start.56
  582.4 2.0 copy-start.61
  584.4 2.8 copy-start.69
  584.4 2.9 copy-start.5
  587.2 2.9 copy-start.75
  594.9 4.2 copy-start.6
  601.1 149.7 %reduce-scatter.31.cloned.1.call-start = ((), (), s32[]{:S(2)}) async-start(), calls=%async_computation.22 | async-start | bytes 2359296 | tf_op jit(solution)/shard_map/reduce_scatter | solution.py:272
  601.2 3.9 copy-start.1
  601.2 3.9 copy-start.37
  607.4 2.1 copy-start.7
  608.7 2.9 copy-start.16
  611.6 226.6 %reduce-scatter.29.cloned.1.call-start = ((), (), s32[]{:S(2)}) async-start(), calls=%async_computation.21 | async-start | bytes 4718592 | tf_op jit(solution)/shard_map/reduce_scatter | solution.py:269
  620.1 306.0 %reduce-scatter.35.cloned.1.call-start = ((), (), s32[]{:S(2)}) async-start(), calls=%async_computation.24 | async-start | bytes 4718592 | tf_op jit(solution)/shard_map/reduce_scatter | solution.py:278
  624.7 402.9 %reduce-scatter.41.cloned.1.call-start = ((), (), s32[]{:S(2)}) async-start(), calls=%async_computation.27 | async-start | bytes 7077888 | tf_op jit(solution)/shard_map/reduce_scatter | solution.py:287
  632.2 496.2 %reduce-scatter.53.cloned.1.call-start = ((), (), s32[]{:S(2)}) async-start(), calls=%async_computation.33 | async-start | bytes 7077888
  646.8 582.0 %reduce-scatter.51.cloned.1.call-start = ((), (), s32[]{:S(2)}) async-start(), calls=%async_computation.32 | async-start | bytes 7077888
  661.5 646.3 %reduce-scatter.47.cloned.1.call-start = ((), (), s32[]{:S(2)}) async-start(), calls=%async_computation.30 | async-start | bytes 278528
  675.1 672.7 %reduce-scatter.45.cloned.1.call-start = ((), (), s32[]{:S(2)}) async-start(), calls=%async_computation.29 | async-start | bytes 278528
  752.6 656.3 %reduce-scatter.43.cloned.1.call-start = ((), (), s32[]{:S(2)}) async-start(), calls=%async_computation.28 | async-start | bytes 557056
  840.4 630.0 %reduce-scatter.49.cloned.1.call-start = ((), (), s32[]{:S(2)}) async-start(), calls=%async_computation.31 | async-start | bytes 557056
  928.2 604.2 %reduce-scatter.55.cloned.1.call-start = ((), (), s32[]{:S(2)}) async-start(), calls=%async_computation.34 | async-start | bytes 835584
  1029.9 202.6 %copy-start.59 = (f32[1024]{0:T(1024)S(1)}, f32[1024]{0:T(1024)}, u32[]{:S(2)}) copy-start(f32[1024]{0:T(1024)} %get-tuple-element.122) | copy-start | bytes 12292
  1029.9 202.6 %copy-start.70 = (f32[1024]{0:T(1024)S(1)}, f32[1024]{0:T(1024)}, u32[]{:S(2)}) copy-start(f32[1024]{0:T(1024)} %get-tuple-element.116) | copy-start | bytes 12292
  1029.9 202.6 %copy-start.71 = (f32[128]{0:T(128)S(1)}, f32[128]{0:T(128)}, u32[]{:S(2)}) copy-start(f32[128]{0:T(128)} %get-tuple-element.118) | copy-start | bytes 1540
  1029.9 564.2 %reduce-scatter.39.cloned.1.call-start = ((), (), s32[]{:S(2)}) async-start(), calls=%async_computation.26 | async-start | bytes 835584 | tf_op jit(solution)/shard_map/reduce_scatter | solution.py:307
  1130.6 525.3 %reduce-scatter.37.cloned.1.call-start = ((), (), s32[]{:S(2)}) async-start(), calls=%async_computation.25 | async-start | bytes 835584 | tf_op jit(solution)/shard_map/reduce_scatter | solution.py:304
  1300.4 3.6 copy-start.13
  1300.4 3.6 copy-start.18
  1304.1 2.1 copy-start.31
  (42 other events, 51.4 us)
Sparse Core Ops, SparseCore 0:
  30.8 54.3 all-gather.7
  87.4 55.1 all-gather.9
  144.7 70.8 all-gather.11
  217.6 71.2 all-gather.13
  291.0 91.3 all-gather.15
  384.4 91.3 all-gather.17
  478.0 91.3 all-gather.19
  601.3 71.9 reduce-scatter.32
  677.0 73.7 reduce-scatter.30
  754.5 83.7 reduce-scatter.28
  842.6 83.4 reduce-scatter.34
  929.8 97.7 reduce-scatter.40
  1031.4 96.8 reduce-scatter.52
  1132.0 96.7 reduce-scatter.50
  1231.0 55.6 reduce-scatter.46
  1289.1 58.5 reduce-scatter.44
  1349.9 58.9 reduce-scatter.42
  1411.2 59.0 reduce-scatter.48
  1472.7 59.5 reduce-scatter.54
  1534.7 59.4 reduce-scatter.38
  1596.5 59.3 reduce-scatter.36
where the time goes:
time: 1670 us; the launch traced here: 1660 us
  waiting for transfers between devices  1240 us (74%)
  blocking collectives  239 us (14%)
  matrix products  90.7 us (5%)
  local copies, waits for them, and re-layouts  60.4 us (4%)
  other arithmetic  20.1 us (1%)
  between operations  18.4 us (1%)
    unnamed x28, waiting for transfers between devices  415 us
    reduce_scatter x1, waiting for transfers between devices, on_device(): lax.psum_scatter(down_wgrad.astype(jnp.bfloat16), 'fsdp', scatter_dimensi...  99.4 us
    all_gather x1, waiting for transfers between devices, fetch_weights(): lax.all_gather(fetched[4], 'fsdp', axis=1, tiled=True)  87.4 us
    all_gather x1, waiting for transfers between devices, fetch_weights(): lax.all_gather(fetched[5], 'fsdp', axis=1, tiled=True)  87 us
    reduce_scatter x1, waiting for transfers between devices, on_device(): lax.psum_scatter(out_wgrad.astype(jnp.bfloat16), 'fsdp', scatter_dimensio...  85.7 us
    reduce_scatter x1, waiting for transfers between devices, on_device(): lax.psum_scatter(query_wgrad.astype(jnp.bfloat16), 'fsdp', scatter_dimens...  85.6 us
    all_gather x1, waiting for transfers between devices, fetch_weights(): lax.all_gather(fetched[6], 'fsdp', axis=0, tiled=True)  85.3 us
    reduce_scatter x1, waiting for transfers between devices, on_device(): lax.psum_scatter(key_wgrad.astype(jnp.bfloat16), 'fsdp', scatter_dimensio...  75.7 us
  transfers between devices with their start and end apart: 21, of which 18 were waited for; matrix products, arithmetic and copies ran while one was open for 8% of the time, Pallas kernels for 0%

commit v1 on v0

v1 whole, which is shorter than its diff:
```python
import numpy as np
import jax
import jax.numpy as jnp
from jax import lax
from jax.experimental import pallas as pl
from jax.experimental.pallas import tpu as pltpu
from jax.sharding import PartitionSpec as P

MESH = pl.DeviceIdType.MESH
F32, BF = jnp.float32, jnp.bfloat16
D, HD, TOK = 1024, 128, 256
EPS = 1e-6
ROPE_BASE = 1000000.0
MATS = (
    ("q", 256, 128, BF, "xyz"),
    ("kv", 256, 128, BF, "yzx"),
    ("o", 256, 128, BF, "zxy"),
    ("g", 384, 128, BF, "xyz"),
    ("u", 384, 128, BF, "yzx"),
    ("d", 384, 128, BF, "zxy"),
    ("n", 128, 16, F32, "zxy"),
)


def nn(a, b):
    return jnp.dot(a, b, preferred_element_type=F32)


def nt(a, b):
    return lax.dot_general(a, b, (((1,), (1,)), ((), ())), preferred_element_type=F32)


def tn(a, b):
    return lax.dot_general(a, b, (((0,), (0,)), ((), ())), preferred_element_type=F32)


def when(cond, body):
    if cond is None:
        body()
    else:
        pl.when(cond)(body)


class Place:
    def __init__(self):
        dp, fs = lax.axis_index("dp"), lax.axis_index("fsdp")
        self.dp = dp
        self.c = lax.rem(dp, 2)
        self.x = lax.rem(lax.div(dp, 2), 4)
        self.yl = lax.div(dp, 8)
        self.yh = lax.div(fs, 4)
        self.z = lax.rem(fs, 4)
        self.y = self.yh * 2 + self.yl
        self.zi = lax.div(self.z, 2)
        self.own = lax.rem(self.z, 2) == self.c
        self.other = lax.rem(self.z, 2) != self.c

    def device(self, x, y, z, c):
        return (lax.rem(y, 2) * 8 + x * 2 + c, lax.div(y, 2) * 4 + z)

    def step(self, axis, by):
        go = lambda v: lax.rem(v + (by + 4), 4)
        return self.device(
            go(self.x) if axis == "x" else self.x,
            go(self.y) if axis == "y" else self.y,
            go(self.z) if axis == "z" else self.z,
            self.c,
        )

    def sibling(self):
        return self.device(self.x, self.y, self.z, 1 - self.c)

    def at(self, axis, by=0):
        if axis == "z":
            return lax.div(lax.rem(self.z + (by + 4), 4), 2)
        return lax.rem((self.x if axis == "x" else self.y) + (by + 4), 4)


def block_index(cols, rows, cx, cy, cz, half):
    yh, yl = (slice(None), slice(None)) if cy is None else (lax.div(cy, 2), lax.rem(cy, 2))
    rr = slice(None) if half is None else pl.ds(half * (rows // 2), rows // 2)
    cc = slice(None) if cz is None else pl.ds(pl.multiple_of(cz * cols, 128), cols)
    return (yh, yl, slice(None) if cx is None else cx, rr, cc)


def block_shape(cols, rows, cx, cy, cz, half):
    lead = (() if cy is not None else (2, 2)) + (() if cx is not None else (4,))
    return lead + (rows // 2 if half else rows, cols if cz is not None else 2 * cols)


class Matrix:
    def __init__(self, number, ref, place, sems):
        self.number, self.ref, self.place = number, ref, place
        self.name, self.cols, self.rows, self.dtype, self.order = MATS[number]
        self.send, self.gather_recv, self.reduce_recv = sems
        self.bufs = None

    def slot(self, phase, kind):
        return (self.number * 3 + phase) * 4 + kind

    def coords(self, phase, order, v, half, gather):
        cur, done = order[phase], order[:phase]
        out = []
        for axis in "xyz":
            if axis == cur:
                out.append(v)
            elif (axis in done) == gather:
                out.append(None)
            else:
                out.append(self.place.at(axis))
        return (self.cols, self.rows, *out, half)

    def gblock(self, phase, v, half=None):
        return self.ref.at[block_index(*self.coords(phase, self.order, v, half, True))]

    def rblock(self, phase, v, half=None):
        return self.ref.at[block_index(*self.coords(phase, self.order[::-1], v, half, False))]

    def copy(self, src, dst, phase, kind, by, axis, recv):
        k = self.slot(phase, kind)
        return pltpu.make_async_remote_copy(
            src_ref=src,
            dst_ref=dst,
            send_sem=self.send.at[k],
            recv_sem=recv.at[k],
            device_id=self.place.step(axis, by),
            device_id_type=MESH,
        )

    def gcopy(self, phase, kind, v):
        half = None if kind < 2 else kind - 2
        ref = self.gblock(phase, v, half)
        return self.copy(
            ref, ref, phase, kind, 1 if kind % 2 == 0 else -1, self.order[phase], self.gather_recv
        )

    def gather_active(self, phase):
        axis = self.order[phase]
        if axis == "z" or "z" in self.order[:phase]:
            return None
        return self.place.own

    def gather1(self, phase):
        axis = self.order[phase]
        here = self.place.at(axis)

        def body():
            self.gcopy(phase, 0, here).start()
            self.gcopy(phase, 1, here).start()

        when(self.place.own if axis == "z" else self.gather_active(phase), body)

    def gather2(self, phase):
        axis = self.order[phase]
        left, right = self.place.at(axis, -1), self.place.at(axis, 1)

        def body():
            self.gcopy(phase, 0, left).wait_recv()
            self.gcopy(phase, 2, left).start()
            self.gcopy(phase, 1, right).wait_recv()
            self.gcopy(phase, 3, right).start()

        when(self.place.other if axis == "z" else self.gather_active(phase), body)

    def gather3(self, phase):
        axis = self.order[phase]
        far = self.place.at(axis, 2)

        def body():
            self.gcopy(phase, 2, far).wait_recv()
            self.gcopy(phase, 3, far).wait_recv()

        when(self.place.own if axis == "z" else self.gather_active(phase), body)

    def gather_drain(self):
        for phase in range(3):
            axis = self.order[phase]
            here = self.place.at(axis)

            def first(phase=phase, here=here):
                self.gcopy(phase, 0, here).wait_send()
                self.gcopy(phase, 1, here).wait_send()

            def second(phase=phase, here=here):
                self.gcopy(phase, 2, here).wait_send()
                self.gcopy(phase, 3, here).wait_send()

            if axis == "z":
                when(self.place.own, first)
                when(self.place.other, second)
            else:
                def both(first=first, second=second):
                    first()
                    second()

                when(self.gather_active(phase), both)

    def landing(self, phase, kind):
        axis = self.order[::-1][phase]
        whole, half = self.bufs[phase]
        if kind < 2:
            return whole.at[kind]
        if axis == "z":
            ref = whole.at[kind - 2]
            idx = (slice(None),) * (len(ref.shape) - 2) + (pl.ds(0, self.rows // 2),)
            return ref.at[idx]
        return half.at[kind - 2]

    def rcopy(self, phase, kind, v):
        half = None if kind < 2 else kind - 2
        return self.copy(
            self.rblock(phase, v, half),
            self.landing(phase, kind),
            phase,
            kind,
            1 if kind % 2 == 0 else -1,
            self.order[::-1][phase],
            self.reduce_recv,
        )

    def reduce_active(self, phase):
        order = self.order[::-1]
        return self.place.own if "z" in order[:phase] else None

    def add(self, phase, v, half, sources, out=None):
        cols, rows, cx, cy, cz, _ = self.coords(phase, self.order[::-1], v, half, False)
        ny, nx = (4 if cy is None else 1), (4 if cx is None else 1)
        height = rows if half is None else rows // 2
        step = min(64, height)
        first = 0 if half is None else half * height
        cc = slice(None) if cz is None else pl.ds(pl.multiple_of(cz * cols, 128), cols)

        def body(n, carry):
            part = lax.rem(n, height // step)
            m = lax.div(n, height // step)
            iy, ix = lax.div(m, nx), lax.rem(m, nx)
            y = iy if cy is None else cy
            x = ix if cx is None else cx
            lead = ((lax.div(iy, 2), lax.rem(iy, 2)) if cy is None else ()) + (
                (ix,) if cx is None else ()
            )
            idx = (
                lax.div(y, 2),
                lax.rem(y, 2),
                x,
                pl.ds(pl.multiple_of(first + part * step, 8), step),
                cc,
            )
            here = pl.ds(pl.multiple_of(part * step, 8), step)
            total = self.ref[idx].astype(F32)
            for src in sources:
                total = total + src[lead + (here, slice(None))].astype(F32)
            if out is None:
                self.ref[idx] = total.astype(self.dtype)
            else:
                out[here, :] = total
            return carry

        lax.fori_loop(0, ny * nx * (height // step), body, 0)

    def reduce1(self, phase):
        axis = self.order[::-1][phase]
        far = self.place.at(axis, 2)

        def body():
            self.rcopy(phase, 2, far).start()
            self.rcopy(phase, 3, far).start()

        when(self.place.own if axis == "z" else self.reduce_active(phase), body)

    def reduce2(self, phase):
        axis = self.order[::-1][phase]
        left, right = self.place.at(axis, -1), self.place.at(axis, 1)

        def body():
            self.rcopy(phase, 2, right).wait_recv()
            self.add(phase, right, 0, [self.landing(phase, 2)])
            self.rcopy(phase, 0, right).start()
            self.rcopy(phase, 3, left).wait_recv()
            self.add(phase, left, 1, [self.landing(phase, 3)])
            self.rcopy(phase, 1, left).start()

        when(self.place.other if axis == "z" else self.reduce_active(phase), body)

    def reduce3(self, phase, out=None):
        axis = self.order[::-1][phase]
        here = self.place.at(axis)

        def body():
            self.rcopy(phase, 0, here).wait_recv()
            self.rcopy(phase, 1, here).wait_recv()
            self.add(phase, here, None, [self.landing(phase, 0), self.landing(phase, 1)], out)

        when(self.place.own if axis == "z" else self.reduce_active(phase), body)

    def reduce_drain(self):
        for phase in range(3):
            axis = self.order[::-1][phase]
            here = self.place.at(axis)

            def first(phase=phase, here=here):
                self.rcopy(phase, 2, here).wait_send()
                self.rcopy(phase, 3, here).wait_send()

            def second(phase=phase, here=here):
                self.rcopy(phase, 0, here).wait_send()
                self.rcopy(phase, 1, here).wait_send()

            if axis == "z":
                when(self.place.own, first)
                when(self.place.other, second)
            else:
                def both(first=first, second=second):
                    first()
                    second()

                when(self.reduce_active(phase), both)


def reduce_shapes():
    shapes = []
    for name, cols, rows, dtype, order in MATS:
        back = order[::-1]
        for phase in range(3):
            known = set(back[: phase + 1])
            cx, cy, cz = (0 if a in known else None for a in "xyz")
            shapes.append(pltpu.VMEM((2,) + block_shape(cols, rows, cx, cy, cz, False), dtype))
            if back[phase] != "z":
                shapes.append(pltpu.VMEM((2,) + block_shape(cols, rows, cx, cy, cz, True), dtype))
    return shapes


PAIR = 48


def kernel(
    tok, small, inv, wq, wk, wv, wo, wg, wu, wd, cot,
    mixed, tgrad, oq, ok, ov, oo, og, ou, od, on,
    Wq, Wkv, Wo, Wg, Wu, Wd, Wn, *rest,
):
    nbuf = len(reduce_shapes())
    bufs, rest = list(rest[:nbuf]), rest[nbuf:]
    (
        send, grecv, rrecv, lsem, psend, precv,
        st_kv, st_o, st_d, X, H, FG, BG, T, CT, QR, KR, Q, K, V, ATT, BR, HID, ACT, H1, H2,
        COS, SIN, BIAS, ACC, SEND, RECV, TG, TU, GROW, GQK, POSR, DG, GP, GPR, FINC, FINF, FINN, DQ, DK, DV,
    ) = rest
    me = Place()
    c = me.c
    sib = me.sibling()
    mine = pl.multiple_of(c * TOK, TOK)
    theirs = pl.multiple_of((1 - c) * TOK, TOK)
    refs = (Wq, Wkv, Wo, Wg, Wu, Wd, Wn)
    mats = []
    for i, ref in enumerate(refs):
        m = Matrix(i, ref, me, (send, grecv, rrecv))
        m.bufs = []
        for phase in range(3):
            whole = bufs.pop(0)
            half = bufs.pop(0) if m.order[::-1][phase] != "z" else None
            m.bufs.append((whole, half))
        mats.append(m)
    mq, mkv, mo, mg, mu, md, mn = mats

    def pair(k, src, dst):
        return pltpu.make_async_remote_copy(
            src_ref=src, dst_ref=dst, send_sem=psend.at[k], recv_sem=precv.at[k],
            device_id=sib, device_id_type=MESH,
        )

    barrier = pltpu.get_barrier_semaphore()
    for target in [me.step(a, s) for a in "xyz" for s in (1, -1)] + [sib]:
        pl.semaphore_signal(barrier, inc=1, device_id=target, device_id_type=MESH)
    st_kv[:, :128] = wk[...]
    st_kv[:, 128:] = wv[...]
    st_o[...] = wo[...].T
    st_d[...] = wd[...].T
    tok_local = pltpu.make_async_copy(tok, X.at[pl.ds(mine, TOK)], lsem.at[8])
    tok_local.start()
    cot_local = pltpu.make_async_copy(cot, CT, lsem.at[9])
    cot_local.start()
    pl.semaphore_wait(barrier, 7)

    shards = [wq, st_kv, st_o, wg, wu, st_d, small.at[pl.ds(0, 8)]]

    def shard_place(m, core):
        h = m.rows // 2
        return m.ref.at[
            me.yh, me.yl, me.x, pl.ds(pl.multiple_of(core * h, 8), h),
            pl.ds(pl.multiple_of(me.zi * m.cols, 128), m.cols),
        ]

    @pl.when(me.own)
    def _():
        for k, m in enumerate(mats):
            pltpu.make_async_copy(shards[k], shard_place(m, c), lsem.at[k]).start()
        for k, m in enumerate(mats):
            pltpu.make_async_copy(shards[k], shard_place(m, c), lsem.at[k]).wait()
            pair(k, shard_place(m, 1 - c), shard_place(m, 1 - c)).wait_recv()

    @pl.when(me.other)
    def _():
        for k, m in enumerate(mats):
            pair(k, shards[k], shard_place(m, c)).start()
        for k, m in enumerate(mats):
            pair(k, shards[k], shard_place(m, c)).wait_send()

    for m in mats:
        m.gather1(0)
    pos_pair = pair(7, small.at[pl.ds(8, 8)], POSR)
    pos_pair.start()
    tok_pair = pair(8, tok, X.at[pl.ds(mine, TOK)])
    tok_pair.start()
    for m in mats:
        m.gather2(0)
    for m in mats:
        m.gather3(0)
        m.gather1(1)
    for m in mats:
        m.gather2(1)
    for m in mats:
        m.gather3(1)
        m.gather1(2)

    pos_pair.wait()
    lane = lax.broadcasted_iota(jnp.int32, (128, 128), 1)
    row = lax.broadcasted_iota(jnp.int32, (128, 128), 0)
    slots = lax.broadcasted_iota(jnp.int32, (128, 256), 1)
    rows2 = lax.broadcasted_iota(jnp.int32, (128, 256), 0)
    inv_row = jnp.broadcast_to(inv[...][:1], (128, 128))
    for b in range(2):
        for h in range(2):
            mine_row = small[8 + h : 9 + h, :]
            other_row = POSR[h : h + 1, :]
            place_row = jnp.where(c == b, mine_row, other_row)
            places = jnp.broadcast_to(place_row, (128, 128)).T
            angles = places * inv_row
            rs = pl.ds(b * 256 + h * 128, 128)
            COS[rs, :] = jnp.cos(angles)
            sine = jnp.sin(angles)
            SIN[rs, :] = jnp.where(lane < 64, -sine, sine)
            t = rows2 + h * 128
            first = t - jnp.concatenate([places, places], axis=1).astype(jnp.int32)
            allowed = (slots <= t) & (slots >= first)
            BIAS[b, pl.ds(h * 128, 128), :] = jnp.where(allowed, 0.0, -1e30)
    tok_local.wait()
    tok_pair.wait()
    cot_local.wait()

    for m in mats:
        m.gather2(2)
    for m in mats:
        m.gather3(2)

    for j in range(8):
        for r in range(2):
            GROW[r : r + 1, j * 128 : (j + 1) * 128] = (
                Wn[0, j // 4, j % 4, r : r + 1, 0:128] + Wn[0, j // 4, j % 4, 8 + r : 9 + r, 0:128]
            )
    gq = jnp.zeros((8, 128), F32)
    for j in range(8):
        gq = gq + Wn[0, j // 4, j % 4, 0:8, 0:128] + Wn[0, j // 4, j % 4, 8:16, 0:128]
    GQK[...] = gq
    qgain = GQK[2:3, :]
    kgain = GQK[3:4, :]

    def full(ref, f0, cols):
        return ref[f0, :, :, :, cols].reshape(1024, -1)

    def tile(ref, f0, j):
        return ref[f0, lax.div(j, 2), pl.ds(lax.rem(j, 2) * 2, 2), :, :].reshape(256, -1)

    def turn(v):
        return pltpu.roll(v, 64, 1)

    def project(f, carry):
        f0, f1 = lax.div(f, 2), lax.rem(f, 2)
        cols = pl.ds(pl.multiple_of(f1 * 256, 128), 256)
        QR[f] = nn(X[...], full(Wq, f0, cols))
        TG[...] = nn(X[...], full(Wkv, f0, cols))
        KR[f] = TG[:, 0:128]

        def head(n, carry):
            b = n
            rs = pl.ds(pl.multiple_of(b * 256, 256), 256)
            cosine, sine = COS[rs, :], SIN[rs, :]
            for r in range(2):
                v = QR[f, rs, pl.ds(r * 128, 128)]
                v = v * lax.rsqrt(jnp.mean(v * v, axis=-1, keepdims=True) + EPS) * qgain
                Q[f, b, pl.ds(r * 256, 256), :] = (v * cosine + turn(v) * sine).astype(BF)
            v = KR[f, rs, :]
            v = v * lax.rsqrt(jnp.mean(v * v, axis=-1, keepdims=True) + EPS) * kgain
            K[f, b] = (v * cosine + turn(v) * sine).astype(BF)
            V[f, b] = TG[rs, 128:256].astype(BF)
            return carry

        lax.fori_loop(0, 2, head, 0)
        return carry

    lax.fori_loop(0, 4, project, 0)

    scale = HD ** -0.5

    def softmax(f, b, r):
        s = nt(Q[f, b, pl.ds(r * 256, 256), :], K[f, b]) * scale + BIAS[b]
        e = jnp.exp(s - jnp.max(s, axis=-1, keepdims=True))
        return e * (1.0 / jnp.sum(e, axis=-1, keepdims=True))

    def attend(n, carry):
        f, b = lax.div(n, 2), lax.rem(n, 2)
        f0, f1 = lax.div(f, 2), lax.rem(f, 2)
        rs = pl.ds(pl.multiple_of(b * 256, 256), 256)
        for r in range(2):
            p = softmax(f, b, r).astype(BF)
            o = nn(p, V[f, b])
            ATT[f0, rs, pl.ds(pl.multiple_of(f1 * 256 + r * 128, 128), 128)] = o.astype(BF)
        return carry

    lax.fori_loop(0, 8, attend, 0)

    def pair_sum(base, slot, products):
        def one(j, carry):
            cols = pl.ds(pl.multiple_of(j * 256, 256), 256)
            TG[...] = products(j)
            SEND[:, cols] = TG[pl.ds(theirs, TOK), :].astype(BF)
            ACC[:, cols] = TG[pl.ds(mine, TOK), :]
            pair(base + j, SEND.at[:, cols], RECV.at[slot, :, cols]).start()
            return carry

        lax.fori_loop(0, 4, one, 0)

        def done(j, carry):
            cols = pl.ds(pl.multiple_of(j * 256, 256), 256)
            pair(base + j, SEND.at[:, cols], RECV.at[slot, :, cols]).wait()
            return carry

        lax.fori_loop(0, 4, done, 0)

    CH = 32
    PER = TOK // CH // 4

    def rows_then_send(base, dst, body):
        def piece(j):
            rs = pl.ds(pl.multiple_of(mine + j * 64, 64), 64)
            return pair(base + j, dst.at[rs], dst.at[rs])

        def theirs_piece(j):
            rs = pl.ds(pl.multiple_of(theirs + j * 64, 64), 64)
            return pair(base + j, dst.at[rs], dst.at[rs])

        def outer(j, carry):
            def inner(i, carry):
                at = pl.multiple_of(j * 64 + i * CH, CH)
                body(pl.ds(at, CH), pl.ds(pl.multiple_of(mine + at, CH), CH))
                return carry

            lax.fori_loop(0, PER, inner, 0)
            piece(j).start()
            return carry

        lax.fori_loop(0, 4, outer, 0)

        def done(j, carry):
            piece(j).wait_send()
            theirs_piece(j).wait_recv()
            return carry

        lax.fori_loop(0, 4, done, 0)

    pair_sum(9, 0, lambda j: nt(ATT[0], tile(Wo, 0, j)) + nt(ATT[1], tile(Wo, 1, j)))

    def hidden_rows(rs, abs_rs):
        v = ACC[rs, :] + RECV[0, rs, :].astype(F32)
        BR[rs, :] = v
        n = v * lax.rsqrt(jnp.mean(v * v, axis=-1, keepdims=True) + EPS) * GROW[0:1, :]
        hid = X[abs_rs, :].astype(F32) + n
        HID[rs, :] = hid
        H[abs_rs, :] = hid.astype(BF)

    rows_then_send(13, H, hidden_rows)

    def ffn_tile(n, carry):
        f0 = lax.div(n, 3)
        cols = pl.ds(pl.multiple_of(lax.rem(n, 3) * 256, 256), 256)
        TG[...] = nn(H[...], full(Wg, f0, cols))
        TU[...] = nn(H[...], full(Wu, f0, cols))

        def rowsof(i, carry):
            rs = pl.ds(pl.multiple_of(i * 64, 64), 64)
            g, u = TG[rs, :], TU[rs, :]
            s = 1.0 / (1.0 + jnp.exp(-g))
            silu = g * s
            ACT[f0, rs, cols] = (silu * u).astype(BF)
            H1[f0, rs, cols] = (s * (1.0 + g * (1.0 - s)) * u).astype(BF)
            H2[f0, rs, cols] = silu.astype(BF)
            return carry

        lax.fori_loop(0, 8, rowsof, 0)
        return carry

    lax.fori_loop(0, 6, ffn_tile, 0)
    pair_sum(17, 1, lambda j: nt(ACT[0], tile(Wd, 0, j)) + nt(ACT[1], tile(Wd, 1, j)))

    DG[...] = jnp.zeros_like(DG)

    def rms_back(v, gain, dn, at):
        r = lax.rsqrt(jnp.mean(v * v, axis=-1, keepdims=True) + EPS)
        gd = gain * dn
        vr = v * r
        grad = r * (gd - vr * jnp.mean(gd * vr, axis=-1, keepdims=True))
        dg = dn * vr
        DG[at, :, :] += jnp.sum(dg.reshape(CH // 8, 8, 1024), axis=0)
        return grad

    def ffn_rows(rs, abs_rs):
        v = ACC[rs, :] + RECV[1, rs, :].astype(F32)
        gain = GROW[1:2, :]
        r = lax.rsqrt(jnp.mean(v * v, axis=-1, keepdims=True) + EPS)
        mixed[rs, :] = (HID[rs, :] + v * r * gain).astype(BF)
        FG[abs_rs, :] = rms_back(v, gain, CT[rs, :].astype(F32), 1).astype(BF)

    rows_then_send(21, FG, ffn_rows)

    def transpose_to(src):
        def one(j, carry):
            cols = pl.ds(pl.multiple_of(j * 128, 128), 128)
            T[cols, :] = src[:, cols].T
            return carry

        lax.fori_loop(0, 8, one, 0)

    for m in mats:
        m.gather_drain()

    def weight_grad(ref, f0, cols, rhs):
        def one(j, carry):
            rs = pl.ds(pl.multiple_of(j * 512, 512), 512)
            out = nn(T[rs, :], rhs()).astype(BF)
            ref[f0, j, :, :, cols] = out.reshape(4, 128, out.shape[-1])
            return carry

        lax.fori_loop(0, 2, one, 0)

    transpose_to(FG)

    def ffn_back_tile(n, carry):
        f0 = lax.div(n, 3)
        cols = pl.ds(pl.multiple_of(lax.rem(n, 3) * 256, 256), 256)
        TG[...] = nn(FG[...], full(Wd, f0, cols))

        def rowsof(i, carry):
            rs = pl.ds(pl.multiple_of(i * 64, 64), 64)
            da = TG[rs, :]
            H1[f0, rs, cols] = (da * H1[f0, rs, cols].astype(F32)).astype(BF)
            H2[f0, rs, cols] = (da * H2[f0, rs, cols].astype(F32)).astype(BF)
            return carry

        lax.fori_loop(0, 8, rowsof, 0)
        weight_grad(Wd, f0, cols, lambda: ACT[f0, :, cols])
        return carry

    lax.fori_loop(0, 6, ffn_back_tile, 0)
    md.reduce1(0)

    pair_sum(
        25, 0,
        lambda j: (nt(H1[0], tile(Wg, 0, j)) + nt(H1[1], tile(Wg, 1, j)))
        + (nt(H2[0], tile(Wu, 0, j)) + nt(H2[1], tile(Wu, 1, j))),
    )
    transpose_to(H)

    def gate_up_grad(n, carry):
        f0 = lax.div(n, 3)
        cols = pl.ds(pl.multiple_of(lax.rem(n, 3) * 256, 256), 256)
        weight_grad(Wg, f0, cols, lambda: H1[f0, :, cols])
        weight_grad(Wu, f0, cols, lambda: H2[f0, :, cols])
        return carry

    lax.fori_loop(0, 6, gate_up_grad, 0)
    mg.reduce1(0)
    mu.reduce1(0)
    md.reduce2(0)

    def branch_rows(rs, abs_rs):
        dn = CT[rs, :].astype(F32) + ACC[rs, :] + RECV[0, rs, :].astype(F32)
        HID[rs, :] = dn
        BG[abs_rs, :] = rms_back(BR[rs, :], GROW[0:1, :], dn, 0).astype(BF)

    rows_then_send(29, BG, branch_rows)
    mg.reduce2(0)
    mu.reduce2(0)

    transpose_to(BG)
    DO = FG

    def out_grad(f, carry):
        f0, f1 = lax.div(f, 2), lax.rem(f, 2)
        cols = pl.ds(pl.multiple_of(f1 * 256, 256), 256)
        DO[:, pl.ds(pl.multiple_of(f * 256, 256), 256)] = nn(BG[...], full(Wo, f0, cols)).astype(BF)
        weight_grad(Wo, f0, cols, lambda: ATT[f0, :, cols])
        return carry

    lax.fori_loop(0, 4, out_grad, 0)
    mo.reduce1(0)
    md.reduce3(0)
    md.reduce1(1)

    GP[...] = jnp.zeros_like(GP)

    def head_back(raw, gain, dn, cosine, sine, row_at):
        d = dn * cosine - turn(dn) * sine
        r = lax.rsqrt(jnp.mean(raw * raw, axis=-1, keepdims=True) + EPS)
        gd = gain * d
        vr = raw * r
        GP[pl.ds(row_at, 8), :] += jnp.sum((d * vr).reshape(32, 8, 128), axis=0)
        return (r * (gd - vr * jnp.mean(gd * vr, axis=-1, keepdims=True))).astype(BF)

    QG, KVG = ACT, H1

    def attend_back(n, carry):
        f, b = lax.div(n, 2), lax.rem(n, 2)
        f0, f1 = lax.div(f, 2), lax.rem(f, 2)
        rs = pl.ds(pl.multiple_of(b * 256, 256), 256)
        for r in range(2):
            p = softmax(f, b, r)
            do = DO[rs, pl.ds(pl.multiple_of(f * 256 + r * 128, 128), 128)]
            dp = nt(do, V[f, b])
            ds = (p * (dp - jnp.sum(p * dp, axis=-1, keepdims=True))).astype(BF)
            q = Q[f, b, pl.ds(r * 256, 256), :]
            dv = tn(p.astype(BF), do)
            dk = tn(ds, q)
            DQ[r] = nn(ds, K[f, b]) * scale
            if r == 0:
                DV[...] = dv
                DK[...] = dk
            else:
                DV[...] += dv
                DK[...] += dk
        cosine, sine = COS[rs, :], SIN[rs, :]
        at = pl.multiple_of(f1 * 256, 256)
        for r in range(2):
            QG[f0, rs, pl.ds(pl.multiple_of(at + r * 128, 128), 128)] = head_back(
                QR[f, rs, pl.ds(r * 128, 128)], qgain, DQ[r], cosine, sine, 0
            )
        KVG[f0, rs, pl.ds(at, 128)] = head_back(
            KR[f, rs, :], kgain, DK[...] * scale, cosine, sine, 8
        )
        KVG[f0, rs, pl.ds(pl.multiple_of(at + 128, 128), 128)] = DV[...].astype(BF)
        return carry

    lax.fori_loop(0, 8, attend_back, 0)
    mg.reduce3(0)
    mg.reduce1(1)
    mu.reduce3(0)
    mu.reduce1(1)
    mo.reduce2(0)
    md.reduce2(1)

    pair_sum(
        33, 1,
        lambda j: (nt(QG[0, :, 0:512], tile(Wq, 0, j)) + nt(QG[1, :, 0:512], tile(Wq, 1, j)))
        + (nt(KVG[0, :, 0:512], tile(Wkv, 0, j)) + nt(KVG[1, :, 0:512], tile(Wkv, 1, j))),
    )
    transpose_to(X)

    def qkv_grad(f, carry):
        f0, f1 = lax.div(f, 2), lax.rem(f, 2)
        cols = pl.ds(pl.multiple_of(f1 * 256, 256), 256)
        weight_grad(Wq, f0, cols, lambda: QG[f0, :, cols])
        weight_grad(Wkv, f0, cols, lambda: KVG[f0, :, cols])
        return carry

    lax.fori_loop(0, 4, qkv_grad, 0)
    mq.reduce1(0)
    mkv.reduce1(0)

    def gain_rows(at, row_at):
        total = jnp.sum(DG[at], axis=0, keepdims=True)
        for j in range(8):
            GP[row_at + j : row_at + j + 1, :] = total[:, j * 128 : (j + 1) * 128]

    qsum = jnp.sum(GP[0:8, :], axis=0, keepdims=True)
    ksum = jnp.sum(GP[8:16, :], axis=0, keepdims=True)
    gain_rows(0, 16)
    gain_rows(1, 24)
    GP[0:1, :] = qsum
    GP[8:9, :] = ksum
    gain_pair = pair(37, GP, GPR)
    gain_pair.start()

    def out_rows(i, carry):
        rs = pl.ds(pl.multiple_of(i * CH, CH), CH)
        tgrad[rs, :] = HID[rs, :] + ACC[rs, :] + RECV[1, rs, :].astype(F32)
        return carry

    lax.fori_loop(0, TOK // CH, out_rows, 0)
    gain_pair.wait()
    GPR[...] += GP[...]
    Wn[...] = jnp.zeros_like(Wn)
    for j in range(8):
        for f0 in range(2):
            for f1 in range(2):
                cols = slice(f1 * 128, (f1 + 1) * 128)
                Wn[f0, j // 4, j % 4, 0:1, cols] = GPR[16 + j : 17 + j, :]
                Wn[f0, j // 4, j % 4, 1:2, cols] = GPR[24 + j : 25 + j, :]
                Wn[f0, j // 4, j % 4, 8:9, cols] = GPR[0:1, :]
                Wn[f0, j // 4, j % 4, 9:10, cols] = GPR[8:9, :]
    mn.reduce1(0)

    mq.reduce2(0)
    mkv.reduce2(0)
    mn.reduce2(0)
    for m in (mo, mq, mkv, mn):
        m.reduce3(0)
        m.reduce1(1)
    for m in (mg, mu, mo, mq, mkv, mn):
        m.reduce2(1)
    for m in (md, mg, mu, mo, mq, mkv, mn):
        m.reduce3(1)
        m.reduce1(2)
    for m in (md, mg, mu, mo, mq, mkv, mn):
        m.reduce2(2)

    fins = {m.name: (FINC.at[k] if k < 3 else FINF.at[k - 3]) for k, m in enumerate(mats[:6])}
    fins["n"] = FINN

    def fin_rows(m, core):
        if m.name == "n":
            return fins["n"]
        return fins[m.name].at[pl.ds(pl.multiple_of(core * 64, 64), 64)]

    order = (md, mg, mu, mo, mq, mkv, mn)
    for m in order:
        m.reduce3(2, out=fins[m.name])

        @pl.when(me.own)
        def _(m=m):
            pair(38 + m.number, fin_rows(m, 1 - c), fin_rows(m, 1 - c)).start()

    for m in order:

        @pl.when(me.own)
        def _(m=m):
            pair(38 + m.number, fin_rows(m, 1 - c), fin_rows(m, 1 - c)).wait_send()

        @pl.when(me.other)
        def _(m=m):
            pair(38 + m.number, fin_rows(m, c), fin_rows(m, c)).wait_recv()

    mrows = pl.ds(pl.multiple_of(c * 64, 64), 64)
    oq[...] = FINC[0, mrows, :]
    ok[...] = FINC[1, mrows, 0:128]
    ov[...] = FINC[1, mrows, 128:256]
    oo[...] = FINC[2, mrows, :].T
    og[...] = FINF[0, mrows, :]
    ou[...] = FINF[1, mrows, :]
    od[...] = FINF[2, mrows, :].T
    on[...] = FINN[...]
    for m in mats:
        m.reduce_drain()


def on_device(
    tokens, positions, w_query, w_key, w_value, w_out, w_gate, w_up, w_down,
    query_gain, key_gain, attn_gain, ffn_gain, cotangent,
):
    dp = lax.axis_index("dp")
    core = dp % 2
    zeros = jnp.zeros((128,), F32)
    put = lambda v, at: lax.dynamic_update_slice(zeros, v.astype(F32), (at,))
    small = jnp.concatenate(
        [
            jnp.stack(
                [
                    put(attn_gain, core * 64),
                    put(ffn_gain, core * 64),
                    put(query_gain, dp * 8),
                    put(key_gain, dp * 8),
                ]
            ),
            jnp.zeros((4, 128), F32),
            positions.astype(F32).reshape(2, 128),
            jnp.zeros((6, 128), F32),
        ]
    )
    steps_up = np.arange(0, HD, 2).astype(np.float32) / np.float32(HD)
    inverse = (np.float32(ROPE_BASE) ** (-steps_up)).astype(np.float32)
    inv = jnp.asarray(np.tile(np.concatenate([inverse, inverse])[None], (8, 1)))
    vm = pl.BlockSpec(memory_space=pltpu.VMEM)
    hbm = pl.BlockSpec(memory_space=pl.ANY)
    n = 84
    V = pltpu.VMEM
    gathered = [V((2, 2, 4, rows, 2 * cols), dt) for _, cols, rows, dt, _ in MATS]
    sems = [pltpu.SemaphoreType.DMA((n,))] * 3 + [
        pltpu.SemaphoreType.DMA((10,)),
        pltpu.SemaphoreType.DMA((PAIR,)),
        pltpu.SemaphoreType.DMA((PAIR,)),
    ]
    work = [
        V((64, 256), BF), V((64, 256), BF), V((64, 384), BF),
        V((512, D), BF), V((512, D), BF), V((512, D), BF), V((512, D), BF), V((D, 512), BF),
        V((TOK, D), BF),
        V((4, 512, 256), F32), V((4, 512, 128), F32),
        V((4, 2, 512, 128), BF), V((4, 2, 256, 128), BF), V((4, 2, 256, 128), BF),
        V((2, 512, 512), BF),
        V((TOK, D), F32), V((TOK, D), F32),
        V((2, 512, 768), BF), V((2, 512, 768), BF), V((2, 512, 768), BF),
        V((512, 128), F32), V((512, 128), F32), V((2, 256, 256), F32),
        V((TOK, D), F32), V((TOK, D), BF), V((2, TOK, D), BF),
        V((512, 256), F32), V((512, 256), F32),
        V((8, D), F32), V((8, 128), F32), V((8, 128), F32), V((2, 8, D), F32),
        V((32, 128), F32), V((32, 128), F32),
        V((3, 128, 256), F32), V((3, 128, 384), F32), V((16, 128), F32),
        V((2, 256, 128), F32), V((256, 128), F32), V((256, 128), F32),
    ]
    f = lambda *s: jax.ShapeDtypeStruct(s, F32)
    outs = pl.pallas_call(
        kernel,
        out_shape=(
            jax.ShapeDtypeStruct((TOK, D), BF), f(TOK, D),
            f(64, 256), f(64, 128), f(64, 128), f(256, 64), f(64, 384), f(64, 384), f(384, 64),
            f(16, 128),
        ),
        in_specs=[hbm] + [vm] * 9 + [hbm],
        out_specs=[vm] * 10,
        scratch_shapes=gathered + reduce_shapes() + sems + work,
        compiler_params=pltpu.CompilerParams(
            collective_id=1, has_side_effects=True, vmem_limit_bytes=int(63.5 * 2**20)
        ),
        cost_estimate=pl.CostEstimate(flops=26 * 10**9, bytes_accessed=4 * 10**6, transcendentals=0),
    )(tokens, small, inv, w_query, w_key, w_value, w_out, w_gate, w_up, w_down, cotangent)
    mixed, tgrad, gq, gk, gv, go, gg, gu, gd, gn = outs
    cut = lambda r, at, size: lax.dynamic_slice(gn[r], (at,), (size,))
    return (
        mixed, tgrad, gq, gk, gv, go, gg, gu, gd,
        cut(8, dp * 8, 8), cut(9, dp * 8, 8), cut(0, core * 64, 64), cut(1, core * 64, 64),
    )


def solution(mesh):
    both, w, wt = P(("dp", "fsdp"), None), P("dp", "fsdp"), P("fsdp", "dp")
    return jax.shard_map(
        on_device,
        mesh=mesh,
        in_specs=(both, P(("dp", "fsdp")), w, w, w, wt, w, w, wt, P("dp"), P("dp"), P("dp"), P("dp"), both),
        out_specs=(both, both, w, w, w, wt, w, w, wt, P("dp"), P("dp"), P("dp"), P("dp")),
        check_vma=False,
    )
```

time: 1670 us -> 243 us (0.15)
  waiting for transfers between devices: 1240 us -> 0 us
  blocking collectives: 239 us -> 0 us
  Pallas kernels: 0 us -> 225 us
  matrix products: 90.7 us -> 0 us
  local copies, waits for them, and re-layouts: 60.4 us -> 16.6 us
  other arithmetic: 20.1 us -> 0.01 us
  between operations: 18.4 us -> 0.76 us
    reduce_scatter x7 -> x0, waiting for transfers between devices: 479 us -> none  [the longest x1 99.4 us: on_device(): lax.psum_scatter(down_wgrad.astype(jnp.bfloat16), 'fsdp', scatter_dimensi...]
    unnamed x28 -> x0, waiting for transfers between devices: 415 us -> none
    all_gather x7 -> x0, waiting for transfers between devices: 341 us -> none  [the longest x1 87.4 us: fetch_weights(): lax.all_gather(fetched[4], 'fsdp', axis=1, tiled=True)]
    pallas_call x0 -> x1, Pallas kernels: none -> 225 us  [on_device(): pl.pallas_call(kernel, out_shape=(jax.ShapeDtypeStruct((TOK, D), BF), f(T...]
    all_gather x7 -> x0, blocking collectives: 145 us -> none  [the longest x1 23.4 us: fetch_weights(): lax.all_gather(w_value, 'dp', axis=0, tiled=True)]
    dot_general x26 -> x0, matrix products: 86.5 us -> none  [the longest x1 8.32 us: on_device(): upward = jnp.dot(hidden_low, up_full, preferred_element_type=jnp.float32)]
    unnamed x2 -> x0, blocking collectives: 63.7 us -> none
    unnamed x200 -> x37, local copies, waits for them, and re-layouts: 56.9 us -> 12.5 us
  transfers between devices with their start and end apart: 21 -> 0, of which waited for: 18 -> 0; matrix products, arithmetic and copies ran while one was open for 8% -> 0% of each run, Pallas kernels for 0% -> 0%
where the time goes in v1:
time: 243 us
  Pallas kernels  225 us (93%)
  local copies, waits for them, and re-layouts  16.6 us (7%)
    pallas_call x1, Pallas kernels, on_device(): pl.pallas_call(kernel, out_shape=(jax.ShapeDtypeStruct((TOK, D), BF), f(T...  225 us
    unnamed x37, local copies, waits for them, and re-layouts  12.5 us

profile of v1, /device:TPU:1, one launch (start us, length us, event | category | flops | bytes accessed | tf_op | source)
XLA Modules:
  0.0 242.6 jit_solution(15763528620521679160)
XLA Ops:
  0.7 0.0 copy-start.9
  0.7 0.0 copy-start.10
  0.7 0.0 copy-start.11
  0.7 0.0 copy-start.12
  0.7 0.0 copy-start.5
  0.7 0.6 copy-done.9
  1.3 0.0 copy-done.10
  1.3 0.0 copy-done.11
  1.3 0.0 copy-done.12
  1.4 0.2 dynamic_update_slice.18
  1.6 0.2 dynamic_update_slice.17
  1.9 0.2 dynamic_update_slice.16
  2.1 0.0 copy-start.8
  2.1 0.2 dynamic_update_slice.19
  2.4 0.4 copy-done.8
  2.8 1.2 concatenate.3.small
  4.0 0.0 copy-done.5
  4.0 0.0 copy-start.4
  4.0 0.7 copy.28.wo
  4.8 0.1 copy-done.4
  4.8 0.7 copy.29.wd
  5.6 225.2 %shard_map.246 = (bf16[256,1024]{1,0:T(8,128)(2,1)}, f32[256,1024]{1,0:T(8,128)}, f32[64,256]{1,0:T(8,128)}, f32[64,128]{1,0:T(8,128)}, f32[64,128]{1,0:T(8,128)...) custom-call(bf16[256,1024]{1,0:T(8,128)(2,1)} %tok.1, ...), custom_call_target="tpu_custom_call" | custom-call | flops 25999998976 | bytes 4000000 | tf_op jit(solution)/shard_map/pallas_call | solution.py:917
  230.8 0.0 copy-start
  230.8 0.8 fusion.4
  231.6 0.6 fusion.2
  232.2 0.6 fusion
  232.8 1.6 copy.30
  234.4 1.7 copy.31
  236.1 1.9 copy.43
  237.9 0.0 copy-done
  237.9 0.0 copy-start.3
  237.9 1.0 copy.44
  238.9 0.0 copy-done.3
  238.9 0.0 copy-start.7
  238.9 0.0 copy-start.2
  238.9 0.6 copy.45
  239.5 0.1 copy-done.7
  239.7 0.0 copy-start.6
  239.7 0.6 copy.46
  240.3 0.2 copy-done.6
  240.4 0.6 copy.47
  241.0 0.0 copy-done.2
  241.1 0.0 copy-start.1
  241.1 0.6 copy.48
  241.7 0.3 copy-done.1
  242.0 0.6 copy.49
  (11 shorter events, 0.0 us)
Async XLA Ops:
  0.7 0.7 copy-start.9
  0.7 0.7 copy-start.10
  0.7 0.7 copy-start.11
  0.7 0.7 copy-start.12
  0.7 3.3 %copy-start.5 = (bf16[256,64]{0,1:T(8,128)(2,1)S(1)}, bf16[256,64]{0,1:T(8,128)(2,1)}, u32[]{:S(2)}) copy-start(bf16[256,64]{0,1:T(8,128)(2,1)} %param.20) | copy-start | bytes 98308
  2.1 0.7 copy-start.8
  4.0 0.8 copy-start.4
  230.8 7.1 %copy-start = (f32[256,1024]{1,0:T(8,128)S(1)}, f32[256,1024]{1,0:T(8,128)}, u32[]{:S(2)}) copy-start(f32[256,1024]{1,0:T(8,128)} %get-tuple-element.68) | copy-start | bytes 3145732
  237.9 1.0 copy-start.3
  238.9 0.8 copy-start.7
  238.9 2.1 copy-start.2
  239.7 0.8 copy-start.6
  241.1 0.9 copy-start.1
